TPU v7x, 512 devices: a whole 4x8x8 slice. The times are simulated.
512 devices in a mesh: rep: 32 (over z_lo, x, core), fsdp: 16 (over z_hi, y).
Axes of the slice: x: 4, y: 8, z: 8 (z_hi: 2, z_lo: 4; z = z_hi * 4 + z_lo), core: 2. Of those that a mesh axis runs over, the one named last changes fastest.
Arguments:
- inputs: bfloat16 [32, 8192, 2048], P('rep', 'fsdp'), may hold values from -6 to 6
- key_grads: bfloat16 [32, 8192, 512], P('rep', 'fsdp'), may hold values from -0.08984375 to 0.08984375
- token_ids: int32 [32, 8192], P('rep', 'fsdp'), may hold values from 0 to 128255, as said below
- step: int32 [], replicated, may hold values from 0 to 7
- master: float32 [32, 2048, 512], P('rep', 'fsdp'), may hold values from -0.125 to 0.125
- first_moment: float32 [32, 2048, 512], P('rep', 'fsdp'), may hold values from -3 to 3
- second_moment: float32 [32, 2048, 512], P('rep', 'fsdp'), may hold values from 0.1 to 4
Outputs:
- mixed_master: float32 [32, 2048, 512], P('rep', 'fsdp')
- new_first: float32 [32, 2048, 512], P('rep', 'fsdp')
- new_second: float32 [32, 2048, 512], P('rep', 'fsdp')
- new_keys: bfloat16 [32, 8192, 512], P('rep', 'fsdp')
Inputs may be any that keep to these rules, and one draw needn't show every extreme that they name: `token_ids`: 0 marks a padding token; other ids are ordinary tokens.
All inputs are finite; a program needn't handle non-finite values.
Results may differ from a plain program's by a relative error of at most 0.013.
Values may be sent and summed in bfloat16 or wider, within the bound.
A program may use at most 64 MiB of HBM per device.

v0:
```python
from functools import partial

import jax
import jax.numpy as jnp
from jax import lax
from jax.sharding import PartitionSpec as P


def as_sent(value):
    return jax.tree.map(lambda a: a.astype(jnp.bfloat16) if a.dtype == jnp.float32 else a, value)


def partner(value, axis, distance):
    mask = 2**distance
    pairs = [(source, source ^ mask) for source in range(lax.axis_size(axis))]
    return lax.ppermute(value, axis, pairs)


def adam_step(weights, moment_one, moment_two, gradient, step):
    new_one = 0.9 * moment_one + 0.1 * gradient
    new_two = 0.95 * moment_two + 0.05 * gradient * gradient
    power = (step + 1).astype(jnp.float32)
    corr_one = 1.0 - jnp.power(jnp.float32(0.9), power)
    corr_two = 1.0 - jnp.power(jnp.float32(0.95), power)
    updated = weights - 0.01 * (new_one / corr_one) / (jnp.sqrt(new_two / corr_two) + 1e-08)
    return (updated, new_one, new_two)


def send_updated(payload, bit_number):
    return jax.tree.map(
        lambda part, own: part.astype(own.dtype),
        partner(as_sent(payload), "rep", bit_number),
        payload,
    )


def by_partner(payload, bit_index, bit_count, transfer):
    branches = [partial(transfer, bit_number=number) for number in range(bit_count)]
    return lax.switch(bit_index, branches, payload)


def on_device(inputs, key_grads, token_ids, step, master, first_moment, second_moment):
    features = inputs[0]
    live_rows = (token_ids[0] != 0)[:, None]
    masked_grads = jnp.where(live_rows, key_grads[0], jnp.zeros_like(key_grads[0]))
    bit_count = min(4, 1 + lax.axis_size("rep") // 8)
    bit_index = step % bit_count
    columns = features
    gradient = lax.psum_scatter(
        lax.dot_general(
            columns, masked_grads, (((0,), (0,)), ((), ())), preferred_element_type=jnp.float32
        ).astype(jnp.bfloat16),
        "fsdp",
        scatter_dimension=0,
        tiled=True,
    ).astype(jnp.float32)
    updated, new_first, new_second = adam_step(
        master[0], first_moment[0], second_moment[0], gradient, step
    )
    partner_updated = by_partner(updated, bit_index, bit_count, send_updated)
    mixed_master = 0.5 * (updated + partner_updated)
    params = mixed_master.astype(jnp.bfloat16)
    empty_keys = jnp.zeros((features.shape[0], params.shape[1]), jnp.float32)
    shard_piece = lax.all_gather(params, "fsdp", axis=0, tiled=True)
    columns = lax.slice_in_dim(features, 0, shard_piece.shape[0], axis=1)
    key_total = empty_keys + jnp.dot(columns, shard_piece, preferred_element_type=jnp.float32)
    new_keys = key_total.astype(jnp.bfloat16)
    return (mixed_master[None], new_first[None], new_second[None], new_keys[None])


def solution(mesh):
    in_specs = (
        P("rep", "fsdp", None),
        P("rep", "fsdp", None),
        P("rep", "fsdp"),
        P(),
        P("rep", "fsdp", None),
        P("rep", "fsdp", None),
        P("rep", "fsdp", None),
    )
    out_specs = (
        P("rep", "fsdp", None),
        P("rep", "fsdp", None),
        P("rep", "fsdp", None),
        P("rep", "fsdp", None),
    )
    return jax.shard_map(
        on_device, mesh=mesh, in_specs=in_specs, out_specs=out_specs, check_vma=False
    )
```

profile of v0, /device:TPU:2, one launch (start us, length us, event | category | flops | bytes accessed | tf_op | source)
XLA Modules:
  0.0 374.0 jit_solution(18377892876960742991)
XLA Ops:
  7.2 0.0 copy-start
  7.2 0.0 reduce-scatter.4.cloned.1.call-start
  7.2 0.8 compare_reduce_fusion
  8.1 0.7 copy-done
  8.8 3.7 fusion
  12.5 3.9 %copy.35 = bf16[2048,512]{1,0:T(8,128)(2,1)} copy(bf16[2048,512]{0,1:T(8,128)(2,1)} %fusion) | data formatting | bytes 4194304
  16.4 0.0 copy-start.1
  16.4 0.0 copy-start.2
  16.4 0.0 reduce-scatter.4.cloned.1.call-update
  16.5 0.0 all-gather.2.cloned.1.call-start
  17.2 0.1 copy-done.1
  17.4 0.1 copy.25
  17.6 0.0 copy-done.2
  17.6 0.1 copy.24
  17.8 0.0 copy-done.3
  17.8 0.8 copy.23
  18.6 231.0 %reduce-scatter.4.cloned.1.call-done = bf16[128,512]{1,0:T(8,128)(2,1)} async-done(((bf16[2048,512]{1,0:T(8,128)(2,1)}), bf16[128,512]{1,0:T(8,128)(2,1)}) %reduce-scatter.4.cloned.1.call-update) | async-done | bytes 131088
  249.6 1.0 copy.36
  250.7 1.2 fusion.17
  251.8 7.1 %conditional.4 = (f32[128,512]{0,1:T(8,128)S(1)}) conditional(s32[]{:T(128)} %clamp.3, (f32[128,512]{0,1:T(8,128)S(1)}) %tuple.45, (f32[128,512]{0,1:T(8,128)S(1)}) %tuple.45, (f32[128,512]{0,1:T(8,128)S(1)}) %tuple.45, (f32[128,512]{0,1:T(8,128)S(1)}) %tuple.45), branch_computations={%region_1.2_spmd, %region_2.3_spmd, %region_3.4_spmd, %region_4.5_... | conditional | bytes 1310768
  251.9 0.1 copy.42
  252.0 2.5 collective-permute-start.1
  254.4 4.4 %collective-permute-done.1 = bf16[128,512]{1,0:T(8,128)(2,1)S(1)} collective-permute-done((bf16[128,512]{1,0:T(8,128)(2,1)S(1)}, bf16[128,512]{1,0:T(8,128)(2,1)S(1)}, u32[]{:S(2)}, u32[]{:S(2)}) %collective-permute-start.1) | collective-permute-done | bytes 131104 | tf_op jit(solution)/shard_map/cond/branch_1_fun/ppermute | solution.py:16
  258.8 0.1 copy.38
  258.9 0.7 fusion.18
  259.6 0.0 all-gather.2.cloned.1.call-update
  259.7 0.8 copy.31
  260.5 0.8 copy.32
  261.3 0.8 copy.33
  262.2 101.1 %all-gather.2.cloned.1.call-done = bf16[2048,512]{0,1:T(8,128)(2,1)} async-done(((bf16[128,512]{0,1:T(8,128)(2,1)}), bf16[2048,512]{0,1:T(8,128)(2,1)}) %all-gather.2.cloned.1.call-update) | async-done | bytes 2097168 | tf_op jit(solution)/shard_map/all_gather | solution.py:64
  363.3 2.9 fusion.7
  366.2 1.0 copy.34
  (1 shorter events, 0.0 us)
Async XLA Ops:
  7.2 1.6 copy-start
  7.2 242.5 %reduce-scatter.4.cloned.1.call-start = ((), (), s32[]{:S(2)}) async-start(), calls=%async_computation.2 | async-start | bytes 2228224
  16.4 0.9 copy-start.1
  16.4 1.2 copy-start.2
  16.4 1.3 copy-start.3
  16.5 346.8 %all-gather.2.cloned.1.call-start = ((), (), s32[]{:S(2)}) async-start(), calls=%async_computation.1 | async-start | bytes 2228224 | tf_op jit(solution)/shard_map/all_gather | solution.py:64
  252.0 6.9 %collective-permute-start.1 = (bf16[128,512]{1,0:T(8,128)(2,1)S(1)}, bf16[128,512]{1,0:T(8,128)(2,1)S(1)}, u32[]{:S(2)}, u32[]{:S(2)}) collective-permute-start(bf16[128,512]{1,0:T(8,128)(2,1)S(1)} %copy.42), channel_id=1, source_target_pairs={{0,32},{16,48},{32,0},{48,16},{64,96},{80,112},{96,64},{112,80},{1... | collective-permute-start | bytes 393224 | tf_op jit(solution)/shard_map/cond/branch_1_fun/ppermute | solution.py:16
Sparse Core Ops, SparseCore 0:
  16.6 233.0 reduce-scatter.3
  259.8 103.4 all-gather.1
where the time goes:
time: 374 us
  waiting for transfers between devices  337 us (90%)
  between operations  14.9 us (4%)
  local copies, waits for them, and re-layouts  10.6 us (3%)
  matrix products  6.6 us (2%)
    unnamed x3, waiting for transfers between devices  231 us
    all_gather x1, waiting for transfers between devices, on_device(): shard_piece = lax.all_gather(params, 'fsdp', axis=0, tiled=True)  101 us
    unnamed x17, local copies, waits for them, and re-layouts  10.4 us
  transfers between devices with their start and end apart: 3, of which 3 were waited for; matrix products, arithmetic and copies ran while one was open for 1% of the time, Pallas kernels for 0%

commit v1 on v0

v1 whole, which is shorter than its diff:
```python
import functools
import math

import jax
import jax.numpy as jnp
from jax import lax
from jax.experimental import pallas as pl
from jax.experimental.pallas import tpu as pltpu
from jax.sharding import PartitionSpec as P

MESH = pl.DeviceIdType.MESH
F32, BF16 = jnp.float32, jnp.bfloat16

NY = 8
NC = 2
OWN, OTHER = 0, 1
CW, CCW = 0, 1
PARTNERS = (1, 2, 4, 8)


def kernel(
    inputs, grads, ids, step, master, first, second,
    mixed_out, first_out, second_out, keys_out,
    x, g, idv, gt, part, rs_in, weights, total, keys, z_send, z_in, mate_send, mate_in,
    w_v, m_v, s_v, mixed_v, first_v, second_v,
    load_sem, rs_ssem, rs_rsem, ag_ssem, ag_rsem, z_ssem, z_rsem, mate_ssem, mate_rsem, gz_ssem, gz_rsem, out_sem,
):
    depth = w_v.shape[0]
    width = w_v.shape[1] // NC
    r, f = lax.axis_index("rep"), lax.axis_index("fsdp")
    y, z = lax.rem(f, NY), f // NY

    def at_y(d):
        return (r, z * NY + lax.rem(y + d + NY, NY))

    across = (r, (1 - z) * NY + y)

    def mate(mask):
        return (r + mask - 2 * mask * lax.rem(r // mask, 2), f)

    towards = (at_y(1), at_y(-1))

    loads = {}

    def load(name, source, target):
        loads[name] = pltpu.make_async_copy(source, target, load_sem.at[len(loads)])
        loads[name].start()

    load("g", grads.at[0], g)
    load("ids", ids, idv)
    order = (4, 3, -3, 2, -2, 1, -1, 0)
    for d in order:
        for zz in (OWN, OTHER):
            plane = z if zz == OWN else 1 - z
            column = pl.multiple_of((plane * NY + lax.rem(y + d + NY, NY)) * depth, depth)
            load((d, zz), inputs.at[0, :, pl.ds(column, depth)], x.at[d % NY, :, pl.ds(zz * depth, depth)])
    load("w", master.at[0], w_v)
    load("m", first.at[0], m_v)
    load("s", second.at[0], s_v)

    barrier = pltpu.get_barrier_semaphore()
    peers = [*towards, across, *[mate(mask) for mask in PARTNERS]]
    for peer in peers:
        pl.semaphore_signal(barrier, inc=1, device_id=peer, device_id_type=MESH)

    loads["g"].wait()
    loads["ids"].wait()
    live = (idv[...] != 0).astype(F32)
    gt[...] = (g[...].astype(F32).T * live).astype(BF16)

    sent = []

    def send(source, target, ssem, rsem, device):
        copy = pltpu.make_async_remote_copy(source, target, ssem, rsem, device_id=device, device_id_type=MESH)
        copy.start()
        sent.append(copy)

    def arrived(target, rsem):
        pltpu.make_async_copy(target, target, rsem).wait()

    def partial(d):
        loads[d, OWN].wait()
        loads[d, OTHER].wait()
        product = jnp.dot(gt[...], x[d % NY], preferred_element_type=F32).astype(BF16)
        part[d % NY, OWN] = product[:, :depth]
        part[d % NY, OTHER] = product[:, depth:]

    def piece(d, zz, c):
        return part.at[d % NY, zz, pl.ds(c * width, width)]

    def far_half(way):
        return OTHER if way == CW else OWN

    def rs_step(c, s, zz):
        for way in (CW, CCW):
            if s == 0 and zz != far_half(way):
                continue
            d = (4 - s) if way == CW else (s - 4)
            own = piece(d, zz, c)
            if s > 1 or (s == 1 and zz == far_half(way)):
                arrived(rs_in.at[way, s - 1, zz, c], rs_rsem.at[way, s - 1, zz, c])
                own[...] = (own[...].astype(F32) + rs_in[way, s - 1, zz, c].astype(F32)).astype(BF16)
            send(own, rs_in.at[way, s, zz, c], rs_ssem.at[way, s, zz, c], rs_rsem.at[way, s, zz, c], towards[way])

    def rs_sum(c, zz):
        own = piece(0, zz, c)[...].astype(F32)
        for way in (CW, CCW):
            arrived(rs_in.at[way, 3, zz, c], rs_rsem.at[way, 3, zz, c])
            own = own + rs_in[way, 3, zz, c].astype(F32)
        return own

    def rs_across(c):
        z_send[c] = rs_sum(c, OTHER).astype(BF16)
        send(z_send.at[c], z_in.at[c], z_ssem.at[c], z_rsem.at[c], across)

    def adam(c):
        if c == 0:
            loads["w"].wait()
            loads["m"].wait()
            loads["s"].wait()
        columns = pl.ds(c * width, width)
        own = rs_sum(c, OWN)
        arrived(z_in.at[c], z_rsem.at[c])
        gradient = (own + z_in[c].astype(F32)).T
        new_one = 0.9 * m_v[:, columns] + 0.1 * gradient
        new_two = 0.95 * s_v[:, columns] + 0.05 * gradient * gradient
        power = jnp.full(new_one.shape, step[0] + 1, jnp.int32).astype(F32)
        corr_one = 1.0 - jnp.exp(power * math.log(0.9))
        corr_two = 1.0 - jnp.exp(power * math.log(0.95))
        updated = w_v[:, columns] - 0.01 * (new_one / corr_one) / (jnp.sqrt(new_two / corr_two) + 1e-08)
        mixed_v[:, columns] = updated
        mate_send[c] = updated.astype(BF16)
        for i, mask in enumerate(PARTNERS):
            send(mate_send.at[c], mate_in.at[c, i], mate_ssem.at[c, i], mate_rsem.at[c, i], mate(mask))
        first_v[:, columns] = new_one
        second_v[:, columns] = new_two

    def mix(c):
        columns = pl.ds(c * width, width)
        bit = jnp.full((depth, width), lax.rem(step[0], len(PARTNERS)), jnp.int32)
        theirs = jnp.zeros((depth, width), F32)
        for i in range(len(PARTNERS)):
            arrived(mate_in.at[c, i], mate_rsem.at[c, i])
            theirs = jnp.where(bit == i, mate_in[c, i].astype(F32), theirs)
        mixed = 0.5 * (mixed_v[:, columns] + theirs)
        mixed_v[:, columns] = mixed
        weights[0, c, :depth] = mixed.astype(BF16)
        send(weights.at[0, c, pl.ds(0, depth)], weights.at[0, c, pl.ds(depth, depth)], gz_ssem.at[c], gz_rsem.at[c], across)

    def ag_step(c, s, zz):
        rows = pl.ds(zz * depth, depth)
        for way in (CW, CCW):
            if s == 4 and zz == far_half(way):
                continue
            have = (1 - s) if way == CW else (s - 1)
            if s > 1:
                arrived(weights.at[have % NY, c, rows], ag_rsem.at[way, s - 1, zz, c])
            elif zz == OTHER and way == CW:
                arrived(weights.at[0, c, rows], gz_rsem.at[c])
            there = -s if way == CW else s
            send(weights.at[have % NY, c, rows], weights.at[there % NY, c, rows], ag_ssem.at[way, s, zz, c], ag_rsem.at[way, s, zz, c], towards[way])

    def ag_last(c):
        arrived(weights.at[4, c, pl.ds(OWN * depth, depth)], ag_rsem.at[CW, 4, OWN, c])
        arrived(weights.at[4, c, pl.ds(OTHER * depth, depth)], ag_rsem.at[CCW, 4, OTHER, c])

    def multiply(c, d):
        term = jnp.dot(x[d % NY], weights[d % NY, c], preferred_element_type=F32)
        if d == 0:
            total[c] = term
        else:
            total[c] += term

    outs = []

    def store(source, target):
        copy = pltpu.make_async_copy(source, target, out_sem.at[len(outs)])
        copy.start()
        outs.append(copy)

    partial(4)
    pl.semaphore_wait(barrier, len(peers))
    rs_step(0, 0, OTHER)
    rs_step(0, 0, OWN)
    partial(3)
    partial(-3)
    rs_step(0, 1, OTHER)
    rs_step(0, 1, OWN)
    rs_step(1, 0, OTHER)
    rs_step(1, 0, OWN)
    partial(2)
    partial(-2)
    rs_step(0, 2, OTHER)
    rs_step(0, 2, OWN)
    partial(1)
    partial(-1)
    partial(0)
    rs_step(0, 3, OTHER)
    rs_step(0, 3, OWN)
    rs_step(1, 1, OTHER)
    rs_step(1, 1, OWN)
    rs_across(0)
    rs_step(1, 2, OTHER)
    rs_step(1, 2, OWN)
    adam(0)
    rs_step(1, 3, OTHER)
    rs_step(1, 3, OWN)
    mix(0)
    ag_step(0, 1, OWN)
    rs_across(1)
    ag_step(0, 1, OTHER)
    ag_step(0, 2, OWN)
    adam(1)
    multiply(0, 0)
    ag_step(0, 2, OTHER)
    multiply(0, 1)
    multiply(0, -1)
    ag_step(0, 3, OWN)
    mix(1)
    ag_step(1, 1, OWN)
    store(mixed_v, mixed_out.at[0])
    store(first_v, first_out.at[0])
    store(second_v, second_out.at[0])
    ag_step(0, 3, OTHER)
    multiply(0, 2)
    multiply(0, -2)
    ag_step(0, 4, OWN)
    ag_step(1, 1, OTHER)
    ag_step(1, 2, OWN)
    multiply(1, 0)
    arrived(weights.at[3, 0, pl.ds(OWN * depth, depth)], ag_rsem.at[CCW, 3, OWN, 0])
    ag_step(0, 4, OTHER)
    arrived(weights.at[-3 % NY, 0, pl.ds(OTHER * depth, depth)], ag_rsem.at[CW, 3, OTHER, 0])
    multiply(0, 3)
    multiply(0, -3)
    ag_step(1, 2, OTHER)
    multiply(1, 1)
    multiply(1, -1)
    ag_step(1, 3, OWN)
    ag_last(0)
    multiply(0, 4)
    keys[:, pl.ds(0, width)] = total[0].astype(BF16)
    store(keys.at[:, pl.ds(0, width)], keys_out.at[0, :, pl.ds(0, width)])
    ag_step(1, 3, OTHER)
    multiply(1, 2)
    multiply(1, -2)
    ag_step(1, 4, OWN)
    arrived(weights.at[3, 1, pl.ds(OWN * depth, depth)], ag_rsem.at[CCW, 3, OWN, 1])
    ag_step(1, 4, OTHER)
    arrived(weights.at[-3 % NY, 1, pl.ds(OTHER * depth, depth)], ag_rsem.at[CW, 3, OTHER, 1])
    multiply(1, 3)
    multiply(1, -3)
    ag_last(1)
    multiply(1, 4)
    keys[:, pl.ds(width, width)] = total[1].astype(BF16)
    store(keys.at[:, pl.ds(width, width)], keys_out.at[0, :, pl.ds(width, width)])

    for copy in sent:
        copy.wait_send()
    for copy in outs:
        copy.wait()


def on_device(inputs, key_grads, token_ids, step, master, first_moment, second_moment):
    tokens, features = inputs.shape[1:]
    depth, columns = master.shape[1:]
    width = columns // NC
    any_space = pl.BlockSpec(memory_space=pl.ANY)
    state = jax.ShapeDtypeStruct(master.shape, F32)
    dma = pltpu.SemaphoreType.DMA
    return pl.pallas_call(
        kernel,
        out_shape=(state, state, state, jax.ShapeDtypeStruct((1, tokens, columns), BF16)),
        in_specs=[any_space] * 3 + [pl.BlockSpec(memory_space=pltpu.SMEM)] + [any_space] * 3,
        out_specs=[any_space] * 4,
        scratch_shapes=[
            pltpu.VMEM((NY, tokens, 2 * depth), BF16),
            pltpu.VMEM((tokens, columns), BF16),
            pltpu.VMEM((1, tokens), jnp.int32),
            pltpu.VMEM((columns, tokens), BF16),
            pltpu.VMEM((NY, 2, columns, depth), BF16),
            pltpu.VMEM((2, 4, 2, NC, width, depth), BF16),
            pltpu.VMEM((NY, NC, 2 * depth, width), BF16),
            pltpu.VMEM((NC, tokens, width), F32),
            pltpu.VMEM((tokens, columns), BF16),
            pltpu.VMEM((NC, width, depth), BF16),
            pltpu.VMEM((NC, width, depth), BF16),
            pltpu.VMEM((NC, depth, width), BF16),
            pltpu.VMEM((NC, len(PARTNERS), depth, width), BF16),
            *[pltpu.VMEM((depth, columns), F32) for _ in range(6)],
            dma((24,)),
            dma((2, 4, 2, NC)),
            dma((2, 4, 2, NC)),
            dma((2, 5, 2, NC)),
            dma((2, 5, 2, NC)),
            dma((NC,)),
            dma((NC,)),
            dma((NC, len(PARTNERS))),
            dma((NC, len(PARTNERS))),
            dma((NC,)),
            dma((NC,)),
            dma((8,)),
        ],
        compiler_params=pltpu.CompilerParams(
            collective_id=0, has_side_effects=True, vmem_limit_bytes=60 * 2**20
        ),
        cost_estimate=pl.CostEstimate(
            flops=4 * tokens * features * columns, bytes_accessed=5 * 2**20, transcendentals=0
        ),
        name="grad_adam_keys",
    )(inputs, key_grads, token_ids, step.reshape(1), master, first_moment, second_moment)


def solution(mesh):
    in_specs = (
        P("rep", "fsdp", None),
        P("rep", "fsdp", None),
        P("rep", "fsdp"),
        P(),
        P("rep", "fsdp", None),
        P("rep", "fsdp", None),
        P("rep", "fsdp", None),
    )
    out_specs = (
        P("rep", "fsdp", None),
        P("rep", "fsdp", None),
        P("rep", "fsdp", None),
        P("rep", "fsdp", None),
    )
    return jax.shard_map(
        on_device, mesh=mesh, in_specs=in_specs, out_specs=out_specs, check_vma=False
    )
```

time: 374 us -> 83.7 us (0.22)
  the two profiles are of different devices: /device:TPU:2 before, /device:TPU:8 now
where the time goes in v1:
time: 83.7 us; the launch traced here: 83.5 us
  Pallas kernels  75.3 us (90%)
  local copies, waits for them, and re-layouts  6.88 us (8%)
  between operations  1.29 us (2%)
    pallas_call x1, Pallas kernels, on_device(): pl.pallas_call(kernel, out_shape=(state, state, state, jax.ShapeDtypeStru...  75.3 us
    unnamed x4, local copies, waits for them, and re-layouts  6.88 us

profile of v1, /device:TPU:8, one launch (start us, length us, event | category | flops | bytes accessed | tf_op | source)
XLA Modules:
  0.0 83.5 jit_solution(16869335055480882274)
XLA Ops:
  1.3 75.3 %grad_adam_keys.1 = (f32[1,128,512]{2,1,0:T(8,128)}, f32[1,128,512]{2,1,0:T(8,128)}, f32[1,128,512]{2,1,0:T(8,128)}, bf16[1,512,512]{2,1,0:T(8,128)(2,1)}) custom-call(bf16[1,512,2048]{2,1,0:T(8,128)(2,1)} %inputs.1, bf16[1,512,512]{2,1,0:T(8,128)(2,1)} %grads.1, s32[1,512]{1,0:T(1,128)} %ids.1, s32[1]{0:T(128)} %bitcast.1.step, f32[1,128,512]{2,1,0:T(8,128)} %master.1, ...), custom_call_target="tpu_custom_call" | custom-call | flops 2147483648 | bytes 5242880 | tf_op jit(solution)/shard_map/grad_adam_keys/pallas_call | solution.py:271
  76.6 1.7 %copy.16 = f32[1,128,512]{2,1,0:T(8,128)} copy(f32[1,128,512]{2,1,0:T(8,128)} %get-tuple-element.8) | data formatting | bytes 524288
  78.3 1.7 %copy.17 = f32[1,128,512]{2,1,0:T(8,128)} copy(f32[1,128,512]{2,1,0:T(8,128)} %get-tuple-element.9) | data formatting | bytes 524288
  79.9 1.7 %copy.18 = f32[1,128,512]{2,1,0:T(8,128)} copy(f32[1,128,512]{2,1,0:T(8,128)} %get-tuple-element.10) | data formatting | bytes 524288
  81.6 1.9 %copy.19 = bf16[1,512,512]{2,1,0:T(8,128)(2,1)} copy(bf16[1,512,512]{2,1,0:T(8,128)(2,1)} %get-tuple-element.11) | data formatting | bytes 1048576

commit v2 on v0

v2 whole, which is shorter than its diff:
```python
import functools
import functools
import math

import jax
import jax.numpy as jnp
from jax import lax
from jax.experimental import pallas as pl
from jax.experimental.pallas import tpu as pltpu
from jax.sharding import PartitionSpec as P

MESH = pl.DeviceIdType.MESH
F32, BF16 = jnp.float32, jnp.bfloat16

NY = 8
NC = 4
OWN, OTHER = 0, 1
CW, CCW = 0, 1
PARTNERS = (1, 2, 4, 8)


def kernel(
    masks, inputs, grads, ids, step, master, first, second,
    mixed_v, first_v, second_v, keys,
    x, g, idv, gt, part, rs_in, weights, total, z_send, z_in, mate_send, mate_in, w_v, m_v, s_v,
    load_sem, rs_ssem, rs_rsem, ag_ssem, ag_rsem, z_ssem, z_rsem, mate_ssem, mate_rsem, gz_ssem, gz_rsem,
):
    depth = w_v.shape[0]
    width = w_v.shape[1] // NC
    r, f = lax.axis_index("rep"), lax.axis_index("fsdp")
    y, z = lax.rem(f, NY), f // NY

    def at_y(d):
        return (r, z * NY + lax.rem(y + d + NY, NY))

    across = (r, (1 - z) * NY + y)

    def mate(mask):
        return (r + mask - 2 * mask * lax.rem(r // mask, 2), f)

    towards = (at_y(1), at_y(-1))

    barrier = pltpu.get_barrier_semaphore()
    peers = [*towards, across, *[mate(mask) for mask in masks]]
    for peer in peers:
        pl.semaphore_signal(barrier, inc=1, device_id=peer, device_id_type=MESH)

    loads = {}

    def load(name, source, target):
        loads[name] = pltpu.make_async_copy(source, target, load_sem.at[len(loads)])
        loads[name].start()

    load("g", grads.at[0], g)
    load("ids", ids, idv)
    for d in (4, 3, -3, 2, -2, 1, -1, 0):
        for zz in (OWN, OTHER):
            plane = z if zz == OWN else 1 - z
            column = pl.multiple_of((plane * NY + lax.rem(y + d + NY, NY)) * depth, depth)
            load((d, zz), inputs.at[0, :, pl.ds(column, depth)], x.at[d % NY, :, pl.ds(zz * depth, depth)])
    load("w", master.at[0], w_v)
    load("m", first.at[0], m_v)
    load("s", second.at[0], s_v)

    sent = []

    def send(source, target, ssem, rsem, device):
        copy = pltpu.make_async_remote_copy(source, target, ssem, rsem, device_id=device, device_id_type=MESH)
        copy.start()
        sent.append(copy)

    def arrived(target, rsem):
        pltpu.make_async_copy(target, target, rsem).wait()

    def prepare():
        loads["g"].wait()
        loads["ids"].wait()
        live = (idv[...] != 0).astype(F32)
        gt[...] = (g[...].astype(F32).T * live).astype(BF16)

    def partial(d):
        loads[d, OWN].wait()
        loads[d, OTHER].wait()
        product = jnp.dot(gt[...], x[d % NY], preferred_element_type=F32).astype(BF16)
        part[d % NY, OWN] = product[:, :depth]
        part[d % NY, OTHER] = product[:, depth:]

    def enter():
        pl.semaphore_wait(barrier, len(peers))

    def far_half(way):
        return OTHER if way == CW else OWN

    def rs(s, *pieces):
        for c, zz in pieces:
            for way in (CW, CCW):
                if s == 0 and zz != far_half(way):
                    continue
                d = (4 - s) if way == CW else (s - 4)
                own = part.at[d % NY, zz, pl.ds(c * width, width)]
                if s > 1 or (s == 1 and zz == far_half(way)):
                    arrived(rs_in.at[way, s - 1, zz, c], rs_rsem.at[way, s - 1, zz, c])
                    own[...] = (own[...].astype(F32) + rs_in[way, s - 1, zz, c].astype(F32)).astype(BF16)
                send(own, rs_in.at[way, s, zz, c], rs_ssem.at[way, s, zz, c], rs_rsem.at[way, s, zz, c], towards[way])

    def rs_sum(c, zz):
        own = part[0, zz, pl.ds(c * width, width)].astype(F32)
        for way in (CW, CCW):
            arrived(rs_in.at[way, 3, zz, c], rs_rsem.at[way, 3, zz, c])
            own = own + rs_in[way, 3, zz, c].astype(F32)
        return own

    def rs_across(c):
        z_send[c] = rs_sum(c, OTHER).astype(BF16)
        send(z_send.at[c], z_in.at[c], z_ssem.at[c], z_rsem.at[c], across)

    def adam(c):
        if c == 0:
            loads["w"].wait()
            loads["m"].wait()
            loads["s"].wait()
        columns = pl.ds(c * width, width)
        own = rs_sum(c, OWN)
        arrived(z_in.at[c], z_rsem.at[c])
        gradient = (own + z_in[c].astype(F32)).T
        new_one = 0.9 * m_v[:, columns] + 0.1 * gradient
        new_two = 0.95 * s_v[:, columns] + 0.05 * gradient * gradient
        power = jnp.full(new_one.shape, step[0] + 1, jnp.int32).astype(F32)
        corr_one = 1.0 - jnp.exp(power * math.log(0.9))
        corr_two = 1.0 - jnp.exp(power * math.log(0.95))
        updated = w_v[:, columns] - 0.01 * (new_one / corr_one) / (jnp.sqrt(new_two / corr_two) + 1e-08)
        mate_send[c] = updated.astype(BF16)
        for i, mask in enumerate(masks):
            send(mate_send.at[c], mate_in.at[c, i], mate_ssem.at[c, i], mate_rsem.at[c, i], mate(mask))
        w_v[:, columns] = updated
        first_v[0, :, columns] = new_one
        second_v[0, :, columns] = new_two

    def block(d, c, zz):
        return weights.at[d % NY, c // 2, pl.ds(zz * depth, depth), pl.ds((c % 2) * width, width)]

    def mix(c):
        columns = pl.ds(c * width, width)
        bit = jnp.full((depth, width), lax.rem(step[0], len(PARTNERS)), jnp.int32)
        theirs = None
        for i, mask in enumerate(masks):
            arrived(mate_in.at[c, i], mate_rsem.at[c, i])
            one = mate_in[c, i].astype(F32)
            theirs = one if theirs is None else jnp.where(bit == PARTNERS.index(mask), one, theirs)
        mixed = 0.5 * (w_v[:, columns] + theirs)
        mixed_v[0, :, columns] = mixed
        block(0, c, OWN)[...] = mixed.astype(BF16)
        send(block(0, c, OWN), block(0, c, OTHER), gz_ssem.at[c], gz_rsem.at[c], across)

    def ag(s, *pieces):
        for c, zz in pieces:
            for way in (CW, CCW):
                if s == 4 and zz == far_half(way):
                    continue
                have = (1 - s) if way == CW else (s - 1)
                if s > 1:
                    ag_wait(way, s - 1, c, zz)
                elif zz == OTHER and way == CW:
                    arrived(block(0, c, OTHER), gz_rsem.at[c])
                there = -s if way == CW else s
                send(block(have, c, zz), block(there, c, zz), ag_ssem.at[way, s, zz, c], ag_rsem.at[way, s, zz, c], towards[way])

    waited = set()

    def ag_wait(way, s, c, zz):
        if (way, s, c, zz) not in waited:
            waited.add((way, s, c, zz))
            arrived(block(-s if way == CW else s, c, zz), ag_rsem.at[way, s, zz, c])

    def multiply(pair, *ds):
        for d in ds:
            for c in (2 * pair, 2 * pair + 1):
                for zz in (OWN, OTHER):
                    if d == 4:
                        ag_wait(CW if zz == OWN else CCW, 4, c, zz)
                    elif d != 0:
                        ag_wait(CW if d < 0 else CCW, abs(d), c, zz)
            term = jnp.dot(x[d % NY], weights[d % NY, pair], preferred_element_type=F32)
            if d == 0:
                total[pair] = term
            elif d != 4:
                total[pair] += term
            else:
                keys[0, :, pl.ds(pair * 2 * width, 2 * width)] = (total[pair] + term).astype(BF16)

    w0, o0, w1, o1 = (0, OWN), (0, OTHER), (1, OWN), (1, OTHER)
    w2, o2, w3, o3 = (2, OWN), (2, OTHER), (3, OWN), (3, OTHER)

    prepare()
    partial(4)
    enter()
    rs(0, o0, w0, o1, w1)
    partial(3)
    partial(-3)
    rs(0, o2, w2, o3, w3)
    partial(2)
    partial(-2)
    rs(1, o0, o1, w0, w1)
    partial(1)
    partial(-1)
    partial(0)
    rs(1, o2, o3)
    rs(2, o0, o1, w0, w1)
    rs(1, w2, w3)
    rs(2, o2, o3)
    rs(3, o0, o1, w0, w1)
    rs(2, w2, w3)
    rs_across(0)
    rs_across(1)
    rs(3, o2, o3)
    rs(3, w2, w3)
    adam(0)
    adam(1)
    rs_across(2)
    rs_across(3)
    mix(0)
    ag(1, w0)
    mix(1)
    ag(1, w1)
    adam(2)
    adam(3)
    ag(2, w0, w1)
    ag(1, o0, o1)
    multiply(0, 0)
    mix(2)
    ag(1, w2)
    mix(3)
    ag(1, w3)
    ag(3, w0, w1)
    ag(2, o0, o1)
    multiply(0, 1, -1)
    ag(2, w2, w3)
    ag(4, w0, w1)
    ag(1, o2, o3)
    multiply(1, 0)
    ag(3, o0, o1)
    multiply(0, 2, -2)
    ag(3, w2, w3)
    ag(2, o2, o3)
    multiply(1, 1, -1)
    ag(4, o0, o1)
    multiply(0, 3, -3)
    ag(4, w2, w3)
    ag(3, o2, o3)
    multiply(1, 2, -2)
    multiply(0, 4)
    ag(4, o2, o3)
    multiply(1, 3, -3, 4)
    for copy in sent:
        copy.wait_send()


def store(*refs):
    count = len(refs) // 2
    sem = refs[-1]
    copies = [pltpu.make_async_copy(refs[i], refs[count + i], sem.at[i]) for i in range(count)]
    for copy in copies:
        copy.start()
    for copy in copies:
        copy.wait()


def on_device(inputs, key_grads, token_ids, step, master, first_moment, second_moment):
    tokens, features = inputs.shape[1:]
    depth, columns = master.shape[1:]
    width = columns // NC
    hbm = pl.BlockSpec(memory_space=pltpu.HBM)
    vmem = pl.BlockSpec(memory_space=pltpu.VMEM)
    dma = pltpu.SemaphoreType.DMA
    shapes = [(master.shape, F32)] * 3 + [((1, tokens, columns), BF16)]

    def with_partner(bit, *operands):
        masks = (PARTNERS[bit],)
        results = pl.pallas_call(
            functools.partial(kernel, masks),
            out_shape=[pltpu.VMEM(shape, dtype) for shape, dtype in shapes],
            in_specs=[hbm] * 3 + [pl.BlockSpec(memory_space=pltpu.SMEM)] + [hbm] * 3,
            out_specs=[vmem] * 4,
            scratch_shapes=[
                pltpu.VMEM((NY, tokens, 2 * depth), BF16),
                pltpu.VMEM((tokens, columns), BF16),
                pltpu.VMEM((1, tokens), jnp.int32),
                pltpu.VMEM((columns, tokens), BF16),
                pltpu.VMEM((NY, 2, columns, depth), BF16),
                pltpu.VMEM((2, 4, 2, NC, width, depth), BF16),
                pltpu.VMEM((NY, NC // 2, 2 * depth, 2 * width), BF16),
                pltpu.VMEM((NC // 2, tokens, 2 * width), F32),
                pltpu.VMEM((NC, width, depth), BF16),
                pltpu.VMEM((NC, width, depth), BF16),
                pltpu.VMEM((NC, depth, width), BF16),
                pltpu.VMEM((NC, len(masks), depth, width), BF16),
                *[pltpu.VMEM((depth, columns), F32) for _ in range(3)],
                dma((24,)),
                dma((2, 4, 2, NC)),
                dma((2, 4, 2, NC)),
                dma((2, 5, 2, NC)),
                dma((2, 5, 2, NC)),
                dma((NC,)),
                dma((NC,)),
                dma((NC, len(masks))),
                dma((NC, len(masks))),
                dma((NC,)),
                dma((NC,)),
            ],
            compiler_params=pltpu.CompilerParams(
                collective_id=bit, has_side_effects=True, vmem_limit_bytes=58 * 2**20
            ),
            cost_estimate=pl.CostEstimate(
                flops=4 * tokens * features * columns, bytes_accessed=5 * 2**20, transcendentals=0
            ),
            name="grad_adam_keys",
        )(*operands)
        return pl.pallas_call(
            store,
            out_shape=[jax.ShapeDtypeStruct(shape, dtype) for shape, dtype in shapes],
            in_specs=[vmem] * 4,
            out_specs=[hbm] * 4,
            scratch_shapes=[dma((4,))],
            name="store_results",
        )(*results)

    branches = [functools.partial(with_partner, bit) for bit in range(len(PARTNERS))]
    return lax.switch(
        lax.rem(step, len(PARTNERS)), branches,
        inputs, key_grads, token_ids, step.reshape(1), master, first_moment, second_moment,
    )


def solution(mesh):
    in_specs = (
        P("rep", "fsdp", None),
        P("rep", "fsdp", None),
        P("rep", "fsdp"),
        P(),
        P("rep", "fsdp", None),
        P("rep", "fsdp", None),
        P("rep", "fsdp", None),
    )
    out_specs = (
        P("rep", "fsdp", None),
        P("rep", "fsdp", None),
        P("rep", "fsdp", None),
        P("rep", "fsdp", None),
    )
    return jax.shard_map(
        on_device, mesh=mesh, in_specs=in_specs, out_specs=out_specs, check_vma=False
    )
```

time: 374 us -> 77.3 us (0.21)
  the two profiles are of different devices: /device:TPU:2 before, /device:TPU:12 now
where the time goes in v2:
time: 77.3 us; the launch traced here: 77.1 us
  Pallas kernels  72.3 us (94%)
  local copies, waits for them, and re-layouts  2.89 us (4%)
  between operations  1.47 us (2%)
    pallas_call x1, Pallas kernels, with_partner(): pl.pallas_call(functools.partial(kernel, masks), out_shape=[pltpu.VMEM(sh...  69.9 us
    cond x8, local copies, waits for them, and re-layouts  2.89 us
    pallas_call x1, Pallas kernels, with_partner(): pl.pallas_call(store, out_shape=[jax.ShapeDtypeStruct(shape, dtype) for s...  2.37 us

profile of v2, /device:TPU:12, one launch (start us, length us, event | category | flops | bytes accessed | tf_op | source)
XLA Modules:
  0.0 77.1 jit_solution(3241595961756212676)
XLA Ops:
  1.3 75.6 %conditional.1 = ((f32[1,128,512]{2,1,0:T(8,128)}, f32[1,128,512]{2,1,0:T(8,128)}, f32[1,128,512]{2,1,0:T(8,128)}, bf16[1,512,512]{2,1,0:T(8,128)(2,1)})) conditional(s32[]{:T(128)} %clamp.3, (bf16[1,512,2048]{2,1,0:T(8,128)(2,1)}, bf16[1,512,512]{2,1,0:T(8,128)(2,1)}, s32[1,512]{1,0:T(1,128)}, s32[]{:T(128)}, ...), branch_computations={%region_0.0_spmd, %region_1.0_spmd, %region_2.0_spmd, %region_3.0_... | conditional | flops 2147483648 | bytes 10485880 | solution.py:328
  1.5 69.9 %grad_adam_keys.7 = (f32[1,128,512]{2,1,0:T(8,128)S(1)}, f32[1,128,512]{2,1,0:T(8,128)S(1)}, f32[1,128,512]{2,1,0:T(8,128)S(1)}, bf16[1,512,512]{2,1,0:T(8,128)(2,1)S(1)}) custom-call(bf16[1,512,2048]{2,1,0:T(8,128)(2,1)} %get-tuple-element.155.inputs, bf16[1,512,512]{2,1,0:T(8,128)(2,1)} %get-tuple-element.159.grads, s32[1,512]{1,0:T(1,128)} %get-tuple-element.163.ids, ...), custom_call_target="tpu_custom_call" | custom-call | flops 2147483648 | bytes 5242880 | tf_op jit(solution)/shard_map/cond/branch_3_fun/grad_adam_keys/pallas_call | solution.py:279
  71.4 0.0 copy-start.3
  71.4 0.8 %copy-done.3 = bf16[1,512,512]{2,1,0:T(8,128)(2,1)} copy-done((bf16[1,512,512]{2,1,0:T(8,128)(2,1)}, bf16[1,512,512]{2,1,0:T(8,128)(2,1)S(1)}, u32[]{:S(2)}) %copy-start.3) | copy-done | bytes 524312 | tf_op jit(solution)/shard_map/cond
  72.2 0.0 copy-start.13
  72.2 0.7 copy-done.13
  72.9 0.0 copy-start.14
  72.9 0.7 copy-done.14
  73.6 0.0 copy-start.15
  73.6 0.7 copy-done.15
  74.3 2.4 %store_results.7 = (f32[1,128,512]{2,1,0:T(8,128)}, f32[1,128,512]{2,1,0:T(8,128)}, f32[1,128,512]{2,1,0:T(8,128)}, bf16[1,512,512]{2,1,0:T(8,128)(2,1)}) custom-call(f32[1,128,512]{2,1,0:T(8,128)} %copy-done.13, f32[1,128,512]{2,1,0:T(8,128)} %copy-done.14, f32[1,128,512]{2,1,0:T(8,128)} %copy-done.15, bf16[1,512,512]{2,1,0:T(8,128)(2,1)} %copy-done.3), custom_call_target="tpu_custom_call" | custom-call | tf_op jit(solution)/shard_map/cond/branch_3_fun/store_results/pallas_call | solution.py:318
Async XLA Ops:
  71.4 0.8 %copy-start.3 = (bf16[1,512,512]{2,1,0:T(8,128)(2,1)}, bf16[1,512,512]{2,1,0:T(8,128)(2,1)S(1)}, u32[]{:S(2)}) copy-start(bf16[1,512,512]{2,1,0:T(8,128)(2,1)S(1)} %get-tuple-element.99.refs_3_) | copy-start | bytes 1572868 | tf_op jit(solution)/shard_map/cond
  72.2 0.7 copy-start.13
  72.9 0.7 copy-start.14
  73.6 0.7 copy-start.15

commit v3 on v2

--- a/solution.py
+++ b/solution.py
@@ -17,13 +17,14 @@
 OWN, OTHER = 0, 1
 CW, CCW = 0, 1
 PARTNERS = (1, 2, 4, 8)
+SHARED = ((0, 1), (0,), (0,), (0,))
 
 
 def kernel(
-    masks, inputs, grads, ids, step, master, first, second,
+    mask, shared, inputs, grads, ids, step, master, first, second,
     mixed_v, first_v, second_v, keys,
-    x, g, idv, gt, part, rs_in, weights, total, z_send, z_in, mate_send, mate_in, w_v, m_v, s_v,
-    load_sem, rs_ssem, rs_rsem, ag_ssem, ag_rsem, z_ssem, z_rsem, mate_ssem, mate_rsem, gz_ssem, gz_rsem,
+    x, g, idv, gt, part, rs_in, zf_in, weights, total, z_send, z_in, mate_send, mate_in, w_v, m_v, s_v,
+    load_sem, rs_ssem, rs_rsem, ag_ssem, ag_rsem, z_ssem, z_rsem, mate_ssem, mate_rsem, gz_ssem, gz_rsem, zf_ssem, zf_rsem, fwd_ssem, fwd_rsem,
 ):
     depth = w_v.shape[0]
     width = w_v.shape[1] // NC
@@ -41,7 +42,7 @@
     towards = (at_y(1), at_y(-1))
 
     barrier = pltpu.get_barrier_semaphore()
-    peers = [*towards, across, *[mate(mask) for mask in masks]]
+    peers = [*towards, across, mate(mask)]
     for peer in peers:
         pl.semaphore_signal(barrier, inc=1, device_id=peer, device_id_type=MESH)
 
@@ -114,15 +115,48 @@
         z_send[c] = rs_sum(c, OTHER).astype(BF16)
         send(z_send.at[c], z_in.at[c], z_ssem.at[c], z_rsem.at[c], across)
 
+    last = NC - 1
+    half = width // 2
+
+    def last_piece(d):
+        return part.at[d % NY, OWN, pl.ds(last * width, width)]
+
+    def zf_send(d):
+        send(part.at[d % NY, OTHER, pl.ds(last * width, width)], zf_in.at[d % NY], zf_ssem.at[d % NY], zf_rsem.at[d % NY], across)
+
+    def zf_add(d):
+        arrived(zf_in.at[d % NY], zf_rsem.at[d % NY])
+        own = last_piece(d)
+        own[...] = (own[...].astype(F32) + zf_in[d % NY].astype(F32)).astype(BF16)
+
+    def zf_rs(s):
+        for d in (4,) if s == 0 else (4 - s, s - 4):
+            zf_add(d)
+        for way in (CW, CCW):
+            d = (4 - s) if way == CW else (s - 4)
+            inbox, ssem, rsem = rs_in.at[way, :, OWN, last], rs_ssem.at[way, :, OWN, last], rs_rsem.at[way, :, OWN, last]
+            halved = pl.ds(way * half, half)
+            whole = pl.ds(0, width)
+            if s > 0:
+                rows = halved if s == 1 else whole
+                arrived(inbox.at[s - 1, rows], rsem.at[s - 1])
+                own = last_piece(d).at[rows]
+                own[...] = (own[...].astype(F32) + inbox[s - 1, rows].astype(F32)).astype(BF16)
+            rows = halved if s == 0 else whole
+            send(last_piece(d).at[rows], inbox.at[s, rows], ssem.at[s], rsem.at[s], towards[way])
+
     def adam(c):
-        if c == 0:
-            loads["w"].wait()
-            loads["m"].wait()
-            loads["s"].wait()
+        for name in ("w", "m", "s"):
+            if name in loads:
+                loads.pop(name).wait()
         columns = pl.ds(c * width, width)
+        if c == last:
+            zf_add(0)
         own = rs_sum(c, OWN)
-        arrived(z_in.at[c], z_rsem.at[c])
-        gradient = (own + z_in[c].astype(F32)).T
+        if c != last:
+            arrived(z_in.at[c], z_rsem.at[c])
+            own = own + z_in[c].astype(F32)
+        gradient = own.T
         new_one = 0.9 * m_v[:, columns] + 0.1 * gradient
         new_two = 0.95 * s_v[:, columns] + 0.05 * gradient * gradient
         power = jnp.full(new_one.shape, step[0] + 1, jnp.int32).astype(F32)
@@ -130,56 +164,79 @@
         corr_two = 1.0 - jnp.exp(power * math.log(0.95))
         updated = w_v[:, columns] - 0.01 * (new_one / corr_one) / (jnp.sqrt(new_two / corr_two) + 1e-08)
         mate_send[c] = updated.astype(BF16)
-        for i, mask in enumerate(masks):
-            send(mate_send.at[c], mate_in.at[c, i], mate_ssem.at[c, i], mate_rsem.at[c, i], mate(mask))
+        send(mate_send.at[c], mate_in.at[c], mate_ssem.at[c], mate_rsem.at[c], mate(mask))
         w_v[:, columns] = updated
         first_v[0, :, columns] = new_one
         second_v[0, :, columns] = new_two
 
+    mine = lax.rem(r // mask, 2)
+
+    def columns_of(c):
+        if c // 2 in shared:
+            return pl.ds(pl.multiple_of(lax.rem(mine + c, 2) * width, width), width)
+        return pl.ds((c % 2) * width, width)
+
     def block(d, c, zz):
-        return weights.at[d % NY, c // 2, pl.ds(zz * depth, depth), pl.ds((c % 2) * width, width)]
+        return weights.at[d % NY, c // 2, pl.ds(zz * depth, depth), columns_of(c)]
 
     def mix(c):
         columns = pl.ds(c * width, width)
-        bit = jnp.full((depth, width), lax.rem(step[0], len(PARTNERS)), jnp.int32)
-        theirs = None
-        for i, mask in enumerate(masks):
-            arrived(mate_in.at[c, i], mate_rsem.at[c, i])
-            one = mate_in[c, i].astype(F32)
-            theirs = one if theirs is None else jnp.where(bit == PARTNERS.index(mask), one, theirs)
-        mixed = 0.5 * (w_v[:, columns] + theirs)
+        arrived(mate_in.at[c], mate_rsem.at[c])
+        mixed = 0.5 * (w_v[:, columns] + mate_in[c].astype(F32))
         mixed_v[0, :, columns] = mixed
-        block(0, c, OWN)[...] = mixed.astype(BF16)
+        weights[0, c // 2, :depth, pl.ds((c % 2) * width, width)] = mixed.astype(BF16)
+        if c // 2 not in shared:
+            to_plane(c)
+
+    def to_plane(c):
         send(block(0, c, OWN), block(0, c, OTHER), gz_ssem.at[c], gz_rsem.at[c], across)
+
+    def gz(pair):
+        to_plane(2 * pair)
+
+    waited = set()
+
+    def once(key, target, rsem):
+        if key not in waited:
+            waited.add(key)
+            arrived(target, rsem)
+
+    def ag_wait(d, c, zz):
+        way, s = (CCW, d) if 0 < d < 4 else (CW, -d)
+        if d == 4:
+            way, s = (CW if zz == OWN else CCW), 4
+        if d != 0:
+            once((d, c, zz), block(d, c, zz), ag_rsem.at[way, s, zz, c])
+        elif zz == OTHER:
+            once((d, c, zz), block(d, c, zz), gz_rsem.at[c])
 
     def ag(s, *pieces):
         for c, zz in pieces:
             for way in (CW, CCW):
                 if s == 4 and zz == far_half(way):
                     continue
-                have = (1 - s) if way == CW else (s - 1)
-                if s > 1:
-                    ag_wait(way, s - 1, c, zz)
-                elif zz == OTHER and way == CW:
-                    arrived(block(0, c, OTHER), gz_rsem.at[c])
-                there = -s if way == CW else s
+                have, there = (1 - s, -s) if way == CW else (s - 1, s)
+                ag_wait(have, c, zz)
                 send(block(have, c, zz), block(there, c, zz), ag_ssem.at[way, s, zz, c], ag_rsem.at[way, s, zz, c], towards[way])
 
-    waited = set()
-
-    def ag_wait(way, s, c, zz):
-        if (way, s, c, zz) not in waited:
-            waited.add((way, s, c, zz))
-            arrived(block(-s if way == CW else s, c, zz), ag_rsem.at[way, s, zz, c])
+    def fwd(pair, d, zz):
+        c = 2 * pair
+        ag_wait(d, c, zz)
+        there = block(d, c, zz)
+        send(there, there, fwd_ssem.at[pair, d % NY, zz], fwd_rsem.at[pair, d % NY, zz], mate(mask))
+
+    def fwd_wait(pair, d, zz):
+        if d != 0 or zz == OTHER:
+            arrived(block(d, 2 * pair + 1, zz), fwd_rsem.at[pair, d % NY, zz])
 
     def multiply(pair, *ds):
         for d in ds:
-            for c in (2 * pair, 2 * pair + 1):
-                for zz in (OWN, OTHER):
-                    if d == 4:
-                        ag_wait(CW if zz == OWN else CCW, 4, c, zz)
-                    elif d != 0:
-                        ag_wait(CW if d < 0 else CCW, abs(d), c, zz)
+            for zz in (OWN, OTHER):
+                ag_wait(d, 2 * pair, zz)
+                if pair in shared:
+                    fwd_wait(pair, d, zz)
+                else:
+                    ag_wait(d, 2 * pair + 1, zz)
             term = jnp.dot(x[d % NY], weights[d % NY, pair], preferred_element_type=F32)
             if d == 0:
                 total[pair] = term
@@ -192,65 +249,209 @@
     w2, o2, w3, o3 = (2, OWN), (2, OTHER), (3, OWN), (3, OTHER)
 
     prepare()
-    partial(4)
-    enter()
-    rs(0, o0, w0, o1, w1)
-    partial(3)
-    partial(-3)
-    rs(0, o2, w2, o3, w3)
-    partial(2)
-    partial(-2)
-    rs(1, o0, o1, w0, w1)
-    partial(1)
-    partial(-1)
-    partial(0)
-    rs(1, o2, o3)
-    rs(2, o0, o1, w0, w1)
-    rs(1, w2, w3)
-    rs(2, o2, o3)
-    rs(3, o0, o1, w0, w1)
-    rs(2, w2, w3)
-    rs_across(0)
-    rs_across(1)
-    rs(3, o2, o3)
-    rs(3, w2, w3)
-    adam(0)
-    adam(1)
-    rs_across(2)
-    rs_across(3)
-    mix(0)
-    ag(1, w0)
-    mix(1)
-    ag(1, w1)
-    adam(2)
-    adam(3)
-    ag(2, w0, w1)
-    ag(1, o0, o1)
-    multiply(0, 0)
-    mix(2)
-    ag(1, w2)
-    mix(3)
-    ag(1, w3)
-    ag(3, w0, w1)
-    ag(2, o0, o1)
-    multiply(0, 1, -1)
-    ag(2, w2, w3)
-    ag(4, w0, w1)
-    ag(1, o2, o3)
-    multiply(1, 0)
-    ag(3, o0, o1)
-    multiply(0, 2, -2)
-    ag(3, w2, w3)
-    ag(2, o2, o3)
-    multiply(1, 1, -1)
-    ag(4, o0, o1)
-    multiply(0, 3, -3)
-    ag(4, w2, w3)
-    ag(3, o2, o3)
-    multiply(1, 2, -2)
-    multiply(0, 4)
-    ag(4, o2, o3)
-    multiply(1, 3, -3, 4)
+    if 1 in shared:
+        partial(4)
+        enter()
+        rs(0, o1, w1, o0, o2)
+        partial(-2)
+        partial(-3)
+        rs(0, w0, w2)
+        zf_send(4)
+        zf_send(-3)
+        partial(-1)
+        partial(3)
+        zf_send(3)
+        rs(1, o1, w1)
+        partial(2)
+        rs(1, o0)
+        zf_send(2)
+        partial(1)
+        zf_send(1)
+        rs(1, o2, w0, w2)
+        partial(0)
+        rs(2, o1)
+        zf_send(0)
+        zf_send(-2)
+        zf_send(-1)
+        rs(2, w1, o0)
+        zf_rs(0)
+        rs(2, o2, w0, w2)
+        rs(3, o1, w1, o0)
+        zf_rs(1)
+        rs(3, o2, w0, w2)
+        rs_across(1)
+        rs_across(0)
+        zf_rs(2)
+        rs_across(2)
+        zf_rs(3)
+        adam(1)
+        adam(0)
+        adam(3)
+        adam(2)
+        mix(1)
+        mix(0)
+        gz(0)
+        ag(1, w0)
+        mix(3)
+        mix(2)
+        gz(1)
+        ag(1, w2)
+        ag(2, w0)
+        fwd(0, 1, OWN)
+        fwd(0, -1, OWN)
+        ag(2, w2)
+        fwd(1, -1, OWN)
+        fwd(1, 1, OWN)
+        fwd(0, -2, OWN)
+        ag(1, o0)
+        ag(3, w0)
+        fwd(0, 2, OWN)
+        fwd(0, 0, OTHER)
+        fwd(1, 2, OWN)
+        ag(1, o2)
+        ag(3, w2)
+        fwd(1, 0, OTHER)
+        fwd(1, -2, OWN)
+        multiply(0, 0)
+        ag(2, o0)
+        fwd(0, 1, OTHER)
+        fwd(0, -1, OTHER)
+        fwd(0, 3, OWN)
+        fwd(0, -3, OWN)
+        ag(4, w0)
+        multiply(1, 0)
+        ag(2, o2)
+        fwd(1, 1, OTHER)
+        fwd(1, -1, OTHER)
+        fwd(1, -3, OWN)
+        ag(4, w2)
+        multiply(0, 1)
+        fwd(1, 3, OWN)
+        multiply(0, -1)
+        fwd(0, -2, OTHER)
+        ag(3, o0)
+        fwd(0, 2, OTHER)
+        fwd(0, 4, OWN)
+        multiply(1, 1, -1)
+        fwd(1, 2, OTHER)
+        ag(3, o2)
+        fwd(1, -2, OTHER)
+        fwd(1, 4, OWN)
+        multiply(0, -2, 2)
+        fwd(0, -3, OTHER)
+        ag(4, o0)
+        fwd(0, 3, OTHER)
+        multiply(1, 2, -2)
+        ag(4, o2)
+        fwd(1, -3, OTHER)
+        fwd(1, 3, OTHER)
+        multiply(0, -3, 3)
+        fwd(0, 4, OTHER)
+        multiply(1, -3, 3)
+        fwd(1, 4, OTHER)
+        multiply(0, 4)
+        multiply(1, 4)
+    else:
+        partial(4)
+        enter()
+        rs(0, o0)
+        zf_send(4)
+        rs(0, o1, w0, w2, o2, w1)
+        partial(-1)
+        zf_send(-1)
+        partial(-3)
+        zf_send(-3)
+        partial(3)
+        partial(2)
+        rs(1, o0)
+        partial(0)
+        zf_send(3)
+        rs(1, o1, w2)
+        partial(1)
+        rs(1, o2, w1)
+        zf_send(1)
+        zf_send(2)
+        zf_send(0)
+        partial(-2)
+        zf_send(-2)
+        rs(2, o0)
+        zf_rs(0)
+        rs(2, o1)
+        rs(1, w0)
+        rs(2, w2, o2, w1)
+        rs(3, o0)
+        zf_rs(1)
+        rs(3, o1)
+        rs(2, w0)
+        rs(3, w2, o2, w1)
+        rs_across(0)
+        rs_across(1)
+        zf_rs(2)
+        rs(3, w0)
+        rs_across(2)
+        zf_rs(3)
+        adam(0)
+        adam(1)
+        adam(3)
+        mix(0)
+        adam(2)
+        mix(1)
+        gz(0)
+        ag(1, w0)
+        mix(3)
+        ag(1, w3)
+        mix(2)
+        ag(1, w2)
+        ag(2, w0)
+        fwd(0, 1, OWN)
+        fwd(0, -1, OWN)
+        ag(2, w3, w2)
+        ag(3, w0)
+        fwd(0, 0, OTHER)
+        fwd(0, -2, OWN)
+        fwd(0, 2, OWN)
+        ag(1, o0)
+        ag(3, w3)
+        ag(1, o3)
+        ag(3, w2)
+        fwd(0, -3, OWN)
+        ag(1, o2)
+        multiply(0, 0)
+        ag(2, o0)
+        fwd(0, 1, OTHER)
+        fwd(0, -1, OTHER)
+        multiply(1, 0)
+        fwd(0, 3, OWN)
+        ag(4, w0, w3)
+        ag(2, o3)
+        ag(4, w2)
+        multiply(1, 1)
+        multiply(0, 1)
+        ag(2, o2)
+        multiply(1, -1)
+        fwd(0, 2, OTHER)
+        ag(3, o0)
+        fwd(0, -2, OTHER)
+        multiply(0, -1)
+        fwd(0, 4, OWN)
+        ag(3, o3)
+        multiply(1, 2)
+        multiply(0, 2)
+        fwd(0, 3, OTHER)
+        ag(4, o0)
+        multiply(0, -2)
+        ag(3, o2)
+        multiply(1, -2)
+        fwd(0, -3, OTHER)
+        ag(4, o3)
+        multiply(0, 3)
+        fwd(0, 4, OTHER)
+        multiply(1, -3)
+        ag(4, o2)
+        multiply(1, 3)
+        multiply(0, -3, 4)
+        multiply(1, 4)
+
     for copy in sent:
         copy.wait_send()
 
@@ -271,13 +472,15 @@
     width = columns // NC
     hbm = pl.BlockSpec(memory_space=pltpu.HBM)
     vmem = pl.BlockSpec(memory_space=pltpu.VMEM)
+    any_space = pl.BlockSpec(memory_space=pl.ANY)
     dma = pltpu.SemaphoreType.DMA
     shapes = [(master.shape, F32)] * 3 + [((1, tokens, columns), BF16)]
 
     def with_partner(bit, *operands):
-        masks = (PARTNERS[bit],)
+        mask = PARTNERS[bit]
+        shared = SHARED[bit]
         results = pl.pallas_call(
-            functools.partial(kernel, masks),
+            functools.partial(kernel, mask, shared),
             out_shape=[pltpu.VMEM(shape, dtype) for shape, dtype in shapes],
             in_specs=[hbm] * 3 + [pl.BlockSpec(memory_space=pltpu.SMEM)] + [hbm] * 3,
             out_specs=[vmem] * 4,
@@ -288,12 +491,13 @@
                 pltpu.VMEM((columns, tokens), BF16),
                 pltpu.VMEM((NY, 2, columns, depth), BF16),
                 pltpu.VMEM((2, 4, 2, NC, width, depth), BF16),
+                pltpu.VMEM((NY, width, depth), BF16),
                 pltpu.VMEM((NY, NC // 2, 2 * depth, 2 * width), BF16),
                 pltpu.VMEM((NC // 2, tokens, 2 * width), F32),
                 pltpu.VMEM((NC, width, depth), BF16),
                 pltpu.VMEM((NC, width, depth), BF16),
                 pltpu.VMEM((NC, depth, width), BF16),
-                pltpu.VMEM((NC, len(masks), depth, width), BF16),
+                pltpu.VMEM((NC, depth, width), BF16),
                 *[pltpu.VMEM((depth, columns), F32) for _ in range(3)],
                 dma((24,)),
                 dma((2, 4, 2, NC)),
@@ -302,10 +506,14 @@
                 dma((2, 5, 2, NC)),
                 dma((NC,)),
                 dma((NC,)),
-                dma((NC, len(masks))),
-                dma((NC, len(masks))),
                 dma((NC,)),
                 dma((NC,)),
+                dma((NC,)),
+                dma((NC,)),
+                dma((NY,)),
+                dma((NY,)),
+                dma((NC // 2, NY, 2)),
+                dma((NC // 2, NY, 2)),
             ],
             compiler_params=pltpu.CompilerParams(
                 collective_id=bit, has_side_effects=True, vmem_limit_bytes=58 * 2**20
@@ -315,11 +523,12 @@
             ),
             name="grad_adam_keys",
         )(*operands)
+        results = [pltpu.with_memory_space_constraint(result, pltpu.VMEM) for result in results]
         return pl.pallas_call(
             store,
             out_shape=[jax.ShapeDtypeStruct(shape, dtype) for shape, dtype in shapes],
-            in_specs=[vmem] * 4,
-            out_specs=[hbm] * 4,
+            in_specs=[any_space] * 4,
+            out_specs=[any_space] * 4,
             scratch_shapes=[dma((4,))],
             name="store_results",
         )(*results)

time: 77.3 us -> 68.7 us (0.89)
  the two profiles are of different devices: /device:TPU:12 before, /device:TPU:4 now
where the time goes in v3:
time: 68.7 us; the launch traced here: 68.5 us
  Pallas kernels  66.9 us (97%)
  between operations  1.45 us (2%)
    pallas_call x1, Pallas kernels, with_partner(): pl.pallas_call(functools.partial(kernel, mask, shared), out_shape=[pltpu....  65.8 us

profile of v3, /device:TPU:4, one launch (start us, length us, event | category | flops | bytes accessed | tf_op | source)
XLA Modules:
  0.0 68.5 jit_solution(7590170252081012866)
XLA Ops:
  1.3 67.1 %conditional.1 = ((f32[1,128,512]{2,1,0:T(8,128)}, f32[1,128,512]{2,1,0:T(8,128)}, f32[1,128,512]{2,1,0:T(8,128)}, bf16[1,512,512]{2,1,0:T(8,128)(2,1)})) conditional(s32[]{:T(128)} %clamp.3, (bf16[1,512,2048]{2,1,0:T(8,128)(2,1)}, bf16[1,512,512]{2,1,0:T(8,128)(2,1)}, s32[1,512]{1,0:T(1,128)}, s32[]{:T(128)}, ...), branch_computations={%region_0.0_spmd, %region_1.0_spmd, %region_2.0_spmd, %region_3.0_... | conditional | flops 2147483648 | bytes 5242888 | solution.py:537
  1.3 65.8 %grad_adam_keys.5 = (f32[1,128,512]{2,1,0:T(8,128)S(1)}, f32[1,128,512]{2,1,0:T(8,128)S(1)}, f32[1,128,512]{2,1,0:T(8,128)S(1)}, bf16[1,512,512]{2,1,0:T(8,128)(2,1)S(1)}) custom-call(bf16[1,512,2048]{2,1,0:T(8,128)(2,1)} %get-tuple-element.153.inputs, bf16[1,512,512]{2,1,0:T(8,128)(2,1)} %get-tuple-element.157.grads, s32[1,512]{1,0:T(1,128)} %get-tuple-element.161.ids, ...), custom_call_target="tpu_custom_call" | custom-call | flops 2147483648 | bytes 5242880 | tf_op jit(solution)/shard_map/cond/branch_1_fun/grad_adam_keys/pallas_call | solution.py:482
  67.1 1.1 %store_results.5 = (f32[1,128,512]{2,1,0:T(8,128)}, f32[1,128,512]{2,1,0:T(8,128)}, f32[1,128,512]{2,1,0:T(8,128)}, bf16[1,512,512]{2,1,0:T(8,128)(2,1)}) custom-call(f32[1,128,512]{2,1,0:T(8,128)S(1)} %get-tuple-element.74.refs_0_, f32[1,128,512]{2,1,0:T(8,128)S(1)} %get-tuple-element.75.refs_1_, f32[1,128,512]{2,1,0:T(8,128)S(1)} %get-tuple-element.76.refs_2_, ...), custom_call_target="tpu_custom_call" | custom-call | tf_op jit(solution)/shard_map/cond/branch_1_fun/store_results/pallas_call | solution.py:527

commit v4 on v3

v4 whole, which is shorter than its diff:
```python
import functools
import functools
import math

import jax
import jax.numpy as jnp
from jax import lax
from jax.experimental import pallas as pl
from jax.experimental.pallas import tpu as pltpu
from jax.sharding import PartitionSpec as P

MESH = pl.DeviceIdType.MESH
F32, BF16 = jnp.float32, jnp.bfloat16

NY = 8
NC = 4
OWN, OTHER = 0, 1
CW, CCW = 0, 1
PARTNERS = (1, 2, 4, 8)
SHARED = ((0, 1, 2, 3), (0, 1, 2), (0, 1, 2), (0, 1, 2))


def kernel(
    mask, shared, inputs, grads, ids, step, master, first, second,
    mixed_v, first_v, second_v, keys,
    x, g, idv, gt, part, rs_in, zf_in, weights, total, z_send, z_in, mate_send, mate_in, state, count,
    load_sem, send_sem, rs_sem, ag_sem, z_sem, mate_sem, gz_sem, zf_sem, fwd_sem,
):
    w_v, m_v, s_v = state.at[0], state.at[1], state.at[2]
    depth = w_v.shape[0]
    width = w_v.shape[1] // NC
    r, f = lax.axis_index("rep"), lax.axis_index("fsdp")
    y, z = lax.rem(f, NY), f // NY

    def at_y(d):
        return (r, z * NY + lax.rem(y + d + NY, NY))

    across = (r, (1 - z) * NY + y)

    def mate(mask):
        return (r + mask - 2 * mask * lax.rem(r // mask, 2), f)

    towards = (at_y(1), at_y(-1))

    def load(i, source, target):
        pltpu.make_async_copy(source, target, load_sem.at[i]).start()

    def loaded(i, target):
        pltpu.make_async_copy(target, target, load_sem.at[i]).wait()

    def load_inputs(*ds):
        for d in ds:
            for zz in (OWN, OTHER):
                plane = z if zz == OWN else 1 - z
                column = pl.multiple_of((plane * NY + lax.rem(y + d + NY, NY)) * depth, depth)
                load(d % NY, inputs.at[0, :, pl.ds(column, depth)], x.at[d % NY, :, pl.ds(zz * depth, depth)])

    load(NY, grads.at[0], g)
    load(NY + 1, ids, idv)
    load_inputs(4)
    barrier = pltpu.get_barrier_semaphore()
    peers = [*towards, at_y(2), at_y(-2), across, mate(mask)]
    for peer in peers:
        pl.semaphore_signal(barrier, inc=1, device_id=peer, device_id_type=MESH)
    load_inputs(3, -3, 2, -2, 1, -1, 0)
    load(NY + 2, master.at[0], w_v)
    load(NY + 2, first.at[0], m_v)
    load(NY + 2, second.at[0], s_v)

    sent = []
    waited = set()

    def send(source, target, sem, device):
        copy = pltpu.make_async_remote_copy(source, target, send_sem.at[0], sem, device_id=device, device_id_type=MESH)
        copy.start()
        sent.append(math.prod(source.shape) // depth)

    def wait(rows, sem):
        some = count.at[pl.ds(0, rows)]
        pltpu.make_async_copy(some, some, sem).wait()

    def prepare():
        loaded(NY, g)
        loaded(NY + 1, idv)
        live = (idv[...] != 0).astype(F32)
        gt[...] = (g[...].astype(F32).T * live).astype(BF16)

    def partial(d):
        loaded(d % NY, x.at[d % NY])
        product = jnp.dot(gt[...], x[d % NY], preferred_element_type=F32).astype(BF16)
        part[d % NY, OWN] = product[:, :depth]
        part[d % NY, OTHER] = product[:, depth:]

    def enter():
        pl.semaphore_wait(barrier, len(peers))

    def far_half(way):
        return OTHER if way == CW else OWN

    def rs(s, *pieces):
        for c, zz in pieces:
            if s > 0:
                wait(width if s == 1 else 2 * width, rs_sem.at[s - 1, zz, c])
            for way in (CW, CCW):
                if s == 0 and zz != far_half(way):
                    continue
                d = (4 - s) if way == CW else (s - 4)
                own = part.at[d % NY, zz, pl.ds(c * width, width)]
                if s > 1 or (s == 1 and zz == far_half(way)):
                    own[...] = (own[...].astype(F32) + rs_in[way, s - 1, zz, c].astype(F32)).astype(BF16)
                send(own, rs_in.at[way, s, zz, c], rs_sem.at[s, zz, c], towards[way])

    def rs_sum(c, zz):
        own = part[0, zz, pl.ds(c * width, width)].astype(F32)
        for s in (2, 3) if c == NC - 1 else (3,):
            wait(2 * width, rs_sem.at[s, zz, c])
            for way in (CW, CCW):
                own = own + rs_in[way, s, zz, c].astype(F32)
        return own

    def rs_across(c):
        z_send[c] = rs_sum(c, OTHER).astype(BF16)
        send(z_send.at[c], z_in.at[c], z_sem.at[c], across)

    last = NC - 1
    half = width // 2

    def last_piece(d):
        return part.at[d % NY, OWN, pl.ds(last * width, width)]

    def zf_send(d):
        send(part.at[d % NY, OTHER, pl.ds(last * width, width)], zf_in.at[d % NY], zf_sem.at[abs(d)], across)

    def zf_add(*ds):
        wait(len(ds) * width, zf_sem.at[abs(ds[0])])
        for d in ds:
            own = last_piece(d)
            own[...] = (own[...].astype(F32) + zf_in[d % NY].astype(F32)).astype(BF16)

    def zf_rs(s):
        zf_add(*((4,) if s == 0 else (4 - s, s - 4)))
        if s == 2:
            wait(width, rs_sem.at[0, OWN, last])
            wait(2 * width, rs_sem.at[1, OWN, last])
        for way in (CW, CCW):
            d = (4 - s) if way == CW else (s - 4)
            relay = at_y((2, 1, 2, 1)[s] * (1 if way == CW else -1))
            inbox = rs_in.at[way, :, OWN, last]
            halved = pl.ds(way * half, half)
            if s == 2:
                own = last_piece(d).at[halved]
                own[...] = (own[...].astype(F32) + inbox[0, halved].astype(F32)).astype(BF16)
                own = last_piece(d)
                own[...] = (own[...].astype(F32) + inbox[1].astype(F32)).astype(BF16)
            rows = halved if s == 0 else pl.ds(0, width)
            send(last_piece(d).at[rows], inbox.at[s, rows], rs_sem.at[s, OWN, last], relay)

    def adam(c):
        if "state" not in waited:
            waited.add("state")
            loaded(NY + 2, state)
        columns = pl.ds(c * width, width)
        if c == last:
            zf_add(0)
        own = rs_sum(c, OWN)
        if c != last:
            wait(width, z_sem.at[c])
            own = own + z_in[c].astype(F32)
        gradient = own.T
        new_one = 0.9 * m_v[:, columns] + 0.1 * gradient
        new_two = 0.95 * s_v[:, columns] + 0.05 * gradient * gradient
        power = jnp.full(new_one.shape, step[0] + 1, jnp.int32).astype(F32)
        corr_one = 1.0 - jnp.exp(power * math.log(0.9))
        corr_two = 1.0 - jnp.exp(power * math.log(0.95))
        updated = w_v[:, columns] - 0.01 * (new_one / corr_one) / (jnp.sqrt(new_two / corr_two) + 1e-08)
        mate_send[c] = updated.astype(BF16)
        send(mate_send.at[c], mate_in.at[c], mate_sem.at[c], mate(mask))
        w_v[:, columns] = updated
        first_v[0, :, columns] = new_one
        second_v[0, :, columns] = new_two

    mine = lax.rem(r // mask, 2)

    def rows_of(d, c, zz, start, rows):
        return weights.at[d % NY, c // 2, pl.ds(zz * depth + start, rows), pl.ds((c % 2) * width, width)]

    def ring(d, c, zz):
        if c in shared:
            return rows_of(d, c, zz, pl.multiple_of(mine * (depth // 2), depth // 2), depth // 2)
        return rows_of(d, c, zz, 0, depth)

    def mix(c):
        columns = pl.ds(c * width, width)
        wait(depth, mate_sem.at[c])
        mixed = 0.5 * (w_v[:, columns] + mate_in[c].astype(F32))
        mixed_v[0, :, columns] = mixed
        rows_of(0, c, OWN, 0, depth)[...] = mixed.astype(BF16)
        send(ring(0, c, OWN), ring(0, c, OTHER), gz_sem.at[c], across)

    def once(key, rows, sem):
        if key not in waited:
            waited.add(key)
            wait(rows, sem)

    def ag_wait(d, c, zz):
        rows = depth // 2 if c in shared else depth
        if d != 0:
            once((abs(d), c, zz), rows if d == 4 else 2 * rows, ag_sem.at[abs(d) - 1, zz, c])
        elif zz == OTHER:
            once((0, c, zz), rows, gz_sem.at[c])

    def ag_send(have, there, way, c, zz):
        device = at_y(abs(have - there) * (1 if way == CW else -1))
        send(ring(have, c, zz), ring(there, c, zz), ag_sem.at[abs(there) - 1, zz, c], device)

    def ag(s, *pieces):
        for c, zz in pieces:
            for way in (CW, CCW):
                if s == 4 and zz == far_half(way):
                    continue
                have, there = (1 - s, -s) if way == CW else (s - 1, s)
                ag_wait(have, c, zz)
                ag_send(have, there, way, c, zz)

    def skip(stage, *pieces):
        for c, zz in pieces:
            for way in (CW, CCW):
                sign = -1 if way == CW else 1
                if stage == 1:
                    ag_wait(0, c, zz)
                    ag_send(0, 2 * sign, way, c, zz)
                else:
                    ag_wait(2 * sign, c, zz)
                    if zz != far_half(way):
                        ag_send(2 * sign, 4 * sign, way, c, zz)
            for way in (CW, CCW):
                sign = -1 if way == CW else 1
                if stage == 1:
                    ag_send(0, sign, way, c, zz)
                else:
                    ag_send(2 * sign, 3 * sign, way, c, zz)

    def fwd(c, d, zz):
        ag_wait(d, c, zz)
        there = ring(d, c, zz)
        send(there, there, fwd_sem.at[c // 2, abs(d)], mate(mask))

    def multiply(pair, *ds):
        for d in ds:
            for c in (2 * pair, 2 * pair + 1):
                for zz in (OWN, OTHER):
                    ag_wait(d, c, zz)
            passed = sum(c in shared for c in (2 * pair, 2 * pair + 1)) * (1, 4, 4, 4, 2)[abs(d)]
            if passed:
                once(("passed", pair, abs(d)), passed * (depth // 2), fwd_sem.at[pair, abs(d)])
            term = jnp.dot(x[d % NY], weights[d % NY, pair], preferred_element_type=F32)
            if d == 0:
                total[pair] = term
            elif d != 4:
                total[pair] += term
            else:
                keys[0, :, pl.ds(pair * 2 * width, 2 * width)] = (total[pair] + term).astype(BF16)

    w0, o0, w1, o1 = (0, OWN), (0, OTHER), (1, OWN), (1, OTHER)
    w2, o2, w3, o3 = (2, OWN), (2, OTHER), (3, OWN), (3, OTHER)

    prepare()
    if mask == 1:
        partial(4)
        enter()
        rs(0, o1)
        partial(0)
        rs(0, w1, o2, w0)
        zf_send(0)
        rs(0, w2, o0)
        partial(-2)
        partial(3)
        partial(-3)
        zf_send(3)
        partial(2)
        zf_send(2)
        partial(1)
        rs(1, o1)
        zf_send(4)
        partial(-1)
        rs(1, o2, w1)
        zf_send(-3)
        zf_send(1)
        rs(1, o0, w0)
        zf_send(-2)
        zf_send(-1)
        rs(1, w2)
        rs(2, o1, o2, w1, o0, w0, w2)
        rs(3, o1, o2)
        zf_rs(0)
        rs(3, w1, o0)
        zf_rs(1)
        rs(3, w0, w2)
        rs_across(1)
        rs_across(2)
        zf_rs(3)
        rs_across(0)
        zf_rs(2)
        adam(1)
        adam(2)
        adam(3)
        adam(0)
        mix(1)
        ag(1, w1)
        mix(2)
        ag(1, w2)
        mix(3)
        ag(1, w3)
        mix(0)
        ag(1, w0)
        fwd(1, 1, OWN)
        ag(2, w1)
        fwd(1, -1, OWN)
        ag(2, w2)
        fwd(2, 1, OWN)
        fwd(2, -1, OWN)
        ag(2, w3)
        fwd(3, -1, OWN)
        fwd(3, 1, OWN)
        ag(2, w0)
        fwd(0, -1, OWN)
        skip(1, o1)
        fwd(1, 0, OTHER)
        fwd(0, 1, OWN)
        ag(3, w1)
        fwd(1, 2, OWN)
        fwd(1, -2, OWN)
        skip(1, o2)
        fwd(2, 0, OTHER)
        ag(3, w2)
        fwd(2, -2, OWN)
        fwd(2, 2, OWN)
        skip(1, o3)
        fwd(3, 0, OTHER)
        ag(3, w3)
        fwd(3, 2, OWN)
        fwd(3, -2, OWN)
        fwd(0, 0, OTHER)
        skip(1, o0)
        ag(3, w0)
        fwd(0, 2, OWN)
        fwd(0, -2, OWN)
        fwd(1, -1, OTHER)
        fwd(1, 1, OTHER)
        fwd(1, -3, OWN)
        ag(4, w1)
        fwd(1, 3, OWN)
        fwd(1, 2, OTHER)
        skip(2, o1)
        fwd(1, -2, OTHER)
        multiply(1, 0)
        multiply(0, 0)
        fwd(2, 1, OTHER)
        fwd(2, -1, OTHER)
        ag(4, w2)
        fwd(2, -3, OWN)
        fwd(2, 3, OWN)
        fwd(2, -2, OTHER)
        fwd(2, 2, OTHER)
        skip(2, o2)
        fwd(3, -1, OTHER)
        fwd(3, 1, OTHER)
        ag(4, w3)
        fwd(3, 3, OWN)
        fwd(3, -3, OWN)
        skip(2, o3)
        fwd(3, -2, OTHER)
        fwd(3, 2, OTHER)
        fwd(0, 1, OTHER)
        fwd(0, -1, OTHER)
        ag(4, w0)
        fwd(0, 3, OWN)
        fwd(0, -3, OWN)
        skip(2, o0)
        fwd(1, 4, OWN)
        fwd(0, -2, OTHER)
        fwd(0, 2, OTHER)
        fwd(1, -3, OTHER)
        multiply(1, -1, 1)
        fwd(2, 4, OWN)
        fwd(1, 3, OTHER)
        fwd(2, -3, OTHER)
        multiply(1, -2, 2)
        fwd(3, 4, OWN)
        fwd(1, 4, OTHER)
        fwd(2, 3, OTHER)
        multiply(0, 1, -1)
        fwd(3, -3, OTHER)
        fwd(2, 4, OTHER)
        fwd(3, 3, OTHER)
        multiply(0, -2, 2)
        fwd(0, 4, OWN)
        fwd(0, -3, OTHER)
        fwd(3, 4, OTHER)
        fwd(0, 3, OTHER)
        fwd(0, 4, OTHER)
        multiply(1, -3, 3)
        multiply(0, -3)
        multiply(1, 4)
        multiply(0, 3, 4)
    else:
        partial(4)
        enter()
        rs(0, o1, w1, w0, o2, o0)
        partial(-3)
        rs(0, w2)
        partial(3)
        partial(-1)
        zf_send(3)
        partial(-2)
        partial(0)
        partial(2)
        rs(1, o1, w1)
        zf_send(2)
        zf_send(-1)
        zf_send(-2)
        zf_send(-3)
        rs(1, o2, w0)
        zf_send(0)
        zf_send(4)
        partial(1)
        rs(1, o0, w2)
        zf_send(1)
        rs(2, o1, w1, o2, w0, o0, w2)
        rs(3, o1, w1, o2, w0, o0, w2)
        zf_rs(1)
        rs_across(1)
        rs_across(2)
        zf_rs(0)
        rs_across(0)
        zf_rs(3)
        zf_rs(2)
        adam(1)
        adam(2)
        adam(0)
        mix(1)
        ag(1, w1)
        mix(2)
        ag(1, w2)
        adam(3)
        mix(0)
        ag(1, w0)
        fwd(1, -1, OWN)
        ag(2, w1)
        fwd(1, 1, OWN)
        ag(2, w2)
        fwd(2, 1, OWN)
        fwd(2, -1, OWN)
        mix(3)
        ag(1, w3)
        fwd(0, 1, OWN)
        ag(2, w0)
        fwd(0, -1, OWN)
        skip(1, o1)
        fwd(1, 0, OTHER)
        ag(3, w1)
        fwd(1, 2, OWN)
        fwd(1, -2, OWN)
        skip(1, o2)
        fwd(2, 0, OTHER)
        ag(3, w2)
        fwd(2, 2, OWN)
        fwd(2, -2, OWN)
        skip(1, o0)
        ag(2, w3)
        fwd(0, 0, OTHER)
        ag(3, w0)
        fwd(0, -2, OWN)
        fwd(0, 2, OWN)
        fwd(1, -1, OTHER)
        fwd(1, 1, OTHER)
        fwd(1, -3, OWN)
        fwd(1, 3, OWN)
        ag(4, w1)
        skip(2, o1)
        fwd(1, -2, OTHER)
        fwd(1, 2, OTHER)
        fwd(2, 1, OTHER)
        fwd(2, -1, OTHER)
        ag(4, w2)
        skip(1, o3)
        fwd(2, -3, OWN)
        fwd(2, 2, OTHER)
        multiply(0, 0)
        fwd(2, 3, OWN)
        fwd(2, -2, OTHER)
        multiply(1, 0)
        skip(2, o2)
        fwd(0, -1, OTHER)
        fwd(0, 1, OTHER)
        skip(2, o0)
        ag(3, w3)
        fwd(0, 2, OTHER)
        ag(4, w0)
        fwd(0, 3, OWN)
        fwd(0, -3, OWN)
        fwd(0, -2, OTHER)
        fwd(1, 4, OWN)
        fwd(1, -3, OTHER)
        fwd(1, 3, OTHER)
        fwd(2, 4, OWN)
        fwd(1, 4, OTHER)
        multiply(1, 1, -1)
        skip(2, o3)
        multiply(1, -2)
        fwd(2, -3, OTHER)
        fwd(0, -3, OTHER)
        multiply(1, 2)
        multiply(0, 2)
        fwd(2, 3, OTHER)
        multiply(0, -1, 1)
        ag(4, w3)
        fwd(2, 4, OTHER)
        fwd(0, 4, OWN)
        multiply(0, -2)
        fwd(0, 3, OTHER)
        fwd(0, 4, OTHER)
        multiply(1, -3)
        multiply(0, -3)
        multiply(1, 3, 4)
        multiply(0, 3, 4)

    wait(sum(sent), send_sem.at[0])


def store(*refs):
    count = len(refs) // 2
    sem = refs[-1]
    copies = [pltpu.make_async_copy(refs[i], refs[count + i], sem.at[i]) for i in range(count)]
    for copy in copies:
        copy.start()
    for copy in copies:
        copy.wait()


def on_device(inputs, key_grads, token_ids, step, master, first_moment, second_moment):
    tokens, features = inputs.shape[1:]
    depth, columns = master.shape[1:]
    width = columns // NC
    hbm = pl.BlockSpec(memory_space=pltpu.HBM)
    vmem = pl.BlockSpec(memory_space=pltpu.VMEM)
    any_space = pl.BlockSpec(memory_space=pl.ANY)
    dma = pltpu.SemaphoreType.DMA
    shapes = [(master.shape, F32)] * 3 + [((1, tokens, columns), BF16)]

    def with_partner(bit, *operands):
        mask = PARTNERS[bit]
        shared = SHARED[bit]
        results = pl.pallas_call(
            functools.partial(kernel, mask, shared),
            out_shape=[pltpu.VMEM(shape, dtype) for shape, dtype in shapes],
            in_specs=[hbm] * 3 + [pl.BlockSpec(memory_space=pltpu.SMEM)] + [hbm] * 3,
            out_specs=[vmem] * 4,
            scratch_shapes=[
                pltpu.VMEM((NY, tokens, 2 * depth), BF16),
                pltpu.VMEM((tokens, columns), BF16),
                pltpu.VMEM((1, tokens), jnp.int32),
                pltpu.VMEM((columns, tokens), BF16),
                pltpu.VMEM((NY, 2, columns, depth), BF16),
                pltpu.VMEM((2, 4, 2, NC, width, depth), BF16),
                pltpu.VMEM((NY, width, depth), BF16),
                pltpu.VMEM((NY, NC // 2, 2 * depth, 2 * width), BF16),
                pltpu.VMEM((NC // 2, tokens, 2 * width), F32),
                pltpu.VMEM((NC, width, depth), BF16),
                pltpu.VMEM((NC, width, depth), BF16),
                pltpu.VMEM((NC, depth, width), BF16),
                pltpu.VMEM((NC, depth, width), BF16),
                pltpu.VMEM((3, depth, columns), F32),
                pltpu.VMEM((NC * 32 * depth, depth), BF16),
                dma((NY + 3,)),
                dma((1,)),
                dma((4, 2, NC)),
                dma((4, 2, NC)),
                dma((NC,)),
                dma((NC,)),
                dma((NC,)),
                dma((5,)),
                dma((NC // 2, 5)),
            ],
            compiler_params=pltpu.CompilerParams(
                collective_id=bit, has_side_effects=True, vmem_limit_bytes=58 * 2**20
            ),
            cost_estimate=pl.CostEstimate(
                flops=4 * tokens * features * columns, bytes_accessed=5 * 2**20, transcendentals=0
            ),
            name="grad_adam_keys",
        )(*operands)
        results = [pltpu.with_memory_space_constraint(result, pltpu.VMEM) for result in results]
        return pl.pallas_call(
            store,
            out_shape=[jax.ShapeDtypeStruct(shape, dtype) for shape, dtype in shapes],
            in_specs=[any_space] * 4,
            out_specs=[any_space] * 4,
            scratch_shapes=[dma((4,))],
            name="store_results",
        )(*results)

    branches = [functools.partial(with_partner, bit) for bit in range(len(PARTNERS))]
    return lax.switch(
        lax.rem(step, len(PARTNERS)), branches,
        inputs, key_grads, token_ids, step.reshape(1), master, first_moment, second_moment,
    )


def solution(mesh):
    in_specs = (
        P("rep", "fsdp", None),
        P("rep", "fsdp", None),
        P("rep", "fsdp"),
        P(),
        P("rep", "fsdp", None),
        P("rep", "fsdp", None),
        P("rep", "fsdp", None),
    )
    out_specs = (
        P("rep", "fsdp", None),
        P("rep", "fsdp", None),
        P("rep", "fsdp", None),
        P("rep", "fsdp", None),
    )
    return jax.shard_map(
        on_device, mesh=mesh, in_specs=in_specs, out_specs=out_specs, check_vma=False
    )
```

time: 68.7 us -> 65 us (0.946)
  the two profiles are of different devices: /device:TPU:4 before, /device:TPU:2 now
where the time goes in v4:
time: 65 us; the launch traced here: 64.9 us
  Pallas kernels  63 us (97%)
  between operations  1.47 us (2%)
    pallas_call x1, Pallas kernels, with_partner(): pl.pallas_call(functools.partial(kernel, mask, shared), out_shape=[pltpu....  61.9 us

profile of v4, /device:TPU:2, one launch (start us, length us, event | category | flops | bytes accessed | tf_op | source)
XLA Modules:
  0.0 64.9 jit_solution(14486778643628600576)
XLA Ops:
  1.3 63.4 %conditional.1 = ((f32[1,128,512]{2,1,0:T(8,128)}, f32[1,128,512]{2,1,0:T(8,128)}, f32[1,128,512]{2,1,0:T(8,128)}, bf16[1,512,512]{2,1,0:T(8,128)(2,1)})) conditional(s32[]{:T(128)} %clamp.3, (bf16[1,512,2048]{2,1,0:T(8,128)(2,1)}, bf16[1,512,512]{2,1,0:T(8,128)(2,1)}, s32[1,512]{1,0:T(1,128)}, s32[]{:T(128)}, ...), branch_computations={%region_0.0_spmd, %region_1.0_spmd, %region_2.0_spmd, %region_3.0_... | conditional | flops 2147483648 | bytes 5242888 | solution.py:604
  1.5 61.9 %grad_adam_keys.6 = (f32[1,128,512]{2,1,0:T(8,128)S(1)}, f32[1,128,512]{2,1,0:T(8,128)S(1)}, f32[1,128,512]{2,1,0:T(8,128)S(1)}, bf16[1,512,512]{2,1,0:T(8,128)(2,1)S(1)}) custom-call(bf16[1,512,2048]{2,1,0:T(8,128)(2,1)} %get-tuple-element.154.inputs, bf16[1,512,512]{2,1,0:T(8,128)(2,1)} %get-tuple-element.158.grads, s32[1,512]{1,0:T(1,128)} %get-tuple-element.162.ids, ...), custom_call_target="tpu_custom_call" | custom-call | flops 2147483648 | bytes 5242880 | tf_op jit(solution)/shard_map/cond/branch_2_fun/grad_adam_keys/pallas_call | solution.py:554
  63.4 1.1 %store_results.6 = (f32[1,128,512]{2,1,0:T(8,128)}, f32[1,128,512]{2,1,0:T(8,128)}, f32[1,128,512]{2,1,0:T(8,128)}, bf16[1,512,512]{2,1,0:T(8,128)(2,1)}) custom-call(f32[1,128,512]{2,1,0:T(8,128)S(1)} %get-tuple-element.85.refs_0_, f32[1,128,512]{2,1,0:T(8,128)S(1)} %get-tuple-element.86.refs_1_, f32[1,128,512]{2,1,0:T(8,128)S(1)} %get-tuple-element.87.refs_2_, ...), custom_call_target="tpu_custom_call" | custom-call | tf_op jit(solution)/shard_map/cond/branch_2_fun/store_results/pallas_call | solution.py:594
